TPU v7x, 256 devices: a whole 4x4x8 slice. The times are simulated.
256 devices in a mesh: tm: 32 (over x, y, core), rows: 8 (over z).
Axes of the slice: x: 4, y: 4, z: 8, core: 2. Of those that a mesh axis runs over, the one named last changes fastest.
Arguments:
- latent: bfloat16 [32, 64, 128, 256], P('tm', 'rows'), may hold values from -6 to 6
- gain_one: float32 [256], replicated, may hold values from 0.1 to 1.9
- conv_one: bfloat16 [3, 3, 3, 256, 256], replicated, may hold values from -0.078125 to 0.078125
- gain_two: float32 [256], replicated, may hold values from 0.1 to 1.9
- conv_two: bfloat16 [3, 3, 3, 256, 256], replicated, may hold values from -0.078125 to 0.078125
- up_weight: bfloat16 [3, 3, 256, 128], replicated, may hold values from -0.125 to 0.125
Outputs:
- upsampled: bfloat16 [32, 128, 256, 128], P('tm', 'rows')
All inputs are finite; a program needn't handle non-finite values.
Results may differ from a plain program's by a relative error of at most 0.0054.
Values may be sent and summed in bfloat16 or wider, within the bound.
A program may use at most 64 MiB of HBM per device.

v0:
```python
import jax
import jax.numpy as jnp
from jax import lax
from jax.sharding import PartitionSpec as P


def with_halo(x, sides, width):
    for axis, dim in sides:
        devices, length = (lax.axis_size(axis), x.shape[dim])
        up = [(i, (i + 1) % devices) for i in range(devices - 1)]
        down = [(j, i) for i, j in up]
        last = lax.slice_in_dim(x, length - width, length, axis=dim)
        leading = lax.slice_in_dim(x, 0, width, axis=dim)
        before = lax.ppermute(last, axis, up)
        after = lax.ppermute(leading, axis, down)
        x = jnp.concatenate([before, x, after], axis=dim)
    return x


def from_behind(block, axis, distance):
    devices = range(lax.axis_size(axis))
    route = [(i - distance, i) for i in devices if i - distance in devices]
    return lax.ppermute(block, axis, route)


def norm_silu(values, scales):
    mean_sq = jnp.mean(values * values, axis=-1, keepdims=True)
    return jax.nn.silu(values * lax.rsqrt(mean_sq + 1e-06) * scales)


def rim_rows(source):
    return with_halo(source, (("rows", 1),), 1)


def past_frames(source):
    frames = source.shape[0]
    reach = (frames + 1) // frames
    pieces = [from_behind(source, "tm", distance) for distance in range(reach, 0, -1)]
    joined = jnp.concatenate(pieces, axis=0)
    return jnp.concatenate([joined, source], axis=0)


def widen(hidden):
    return past_frames(rim_rows(hidden))


def column_taps(extended, width):
    padded = jnp.pad(extended, ((0, 0), (0, 0), (1, 1), (0, 0)))
    return jnp.concatenate([padded[:, :, offset : offset + width] for offset in range(3)], axis=-1)


def causal(extended, kernel, frames, height, width):
    channels = kernel.shape[3]
    wide = column_taps(extended, width)
    matrices = kernel.reshape(3, 3, 3 * channels, kernel.shape[4])
    total = None
    for depth_tap in range(3):
        for row_tap in range(3):
            window = wide[depth_tap : depth_tap + frames, row_tap : row_tap + height]
            term = jnp.einsum(
                "frwc,co->frwo",
                window,
                matrices[depth_tap, row_tap],
                preferred_element_type=jnp.float32,
            )
            total = term if total is None else total + term
    return total


def body(latent, gain_one, conv_one, gain_two, conv_two, up_weight):
    frames, height, width, channels = latent.shape
    source = latent.astype(jnp.float32)
    first = norm_silu(source, gain_one).astype(jnp.bfloat16)
    inner = causal(widen(first), conv_one, frames, height, width)
    second = norm_silu(inner, gain_two).astype(jnp.bfloat16)
    block_out = (source + causal(widen(second), conv_two, frames, height, width)).astype(
        jnp.bfloat16
    )
    rimmed = with_halo(block_out, (("rows", 1),), 1)
    grown = jnp.repeat(rimmed, 2, axis=1)[:, 1:-1]
    grown = jnp.repeat(grown, 2, axis=2)
    wide = column_taps(grown, 2 * width)
    matrices = up_weight.reshape(3, 3 * channels, up_weight.shape[3])
    total = None
    for row_tap in range(3):
        window = wide[:, row_tap : row_tap + 2 * height]
        term = jnp.einsum(
            "frwc,co->frwo", window, matrices[row_tap], preferred_element_type=jnp.float32
        )
        total = term if total is None else total + term
    return total.astype(jnp.bfloat16)


def solution(mesh):
    placed = (P("tm", "rows", None, None), P(), P(), P(), P(), P())
    return jax.shard_map(
        body, mesh=mesh, in_specs=placed, out_specs=P("tm", "rows", None, None), check_vma=False
    )
```

profile of v0, /device:TPU:6, one launch (start us, length us, event | category | flops | bytes accessed | tf_op | source)
XLA Modules:
  0.0 122.2 jit_solution(721414749323589536)
XLA Ops:
  0.0 1.3 %fusion.54 = f32[8,128]{1,0:T(8,128)S(1)} fusion(bf16[1,8,128,256]{3,2,1,0:T(8,128)(2,1)} %param.6), kind=kLoop, calls=%fused_computation.89 | loop fusion | flops 785408 | bytes 528384 | tf_op jit(solution)/shard_map/reduce_sum | solution.py:27
  1.3 1.4 %fusion.61 = bf16[1,8,128,256]{3,2,1,0:T(8,128)(2,1)S(1)} fusion(bf16[1,8,128,256]{3,2,1,0:T(8,128)(2,1)} %param.6, f32[256]{0:T(256)} %param.7, f32[8,128]{1,0:T(8,128)S(1)} %add_rsqrt_fusion.1), kind=kLoop, calls=%fused_computation.96 | loop fusion | flops 2097152 | bytes 1053696 | tf_op jit(solution)/shard_map/convert_element_type | solution.py:73
  2.7 3.8 %collective-permute-start = (bf16[1,1,128,256]{3,2,1,0:T(8,128)(2,1)S(1)}, bf16[1,1,128,256]{3,2,1,0:T(8,128)(2,1)S(1)}, u32[]{:S(2)}, u32[]{:S(2)}) collective-permute-start(bf16[1,1,128,256]{3,2,1,0:T(8,128)(2,1)S(1)} %get-tuple-element.18), channel_id=1, source_target_pairs={{0,1},{1,2},{2,3},{3,4},{4,5},{5,6},{6,7},{8,9},{9,10},{10,11},{11... | collective-permute-start | bytes 196616 | tf_op jit(solution)/shard_map/ppermute | solution.py:14
  6.6 1.3 %collective-permute-start.1 = (bf16[1,1,128,256]{3,2,1,0:T(8,128)(2,1)S(1)}, bf16[1,1,128,256]{3,2,1,0:T(8,128)(2,1)S(1)}, u32[]{:S(2)}, u32[]{:S(2)}) collective-permute-start(bf16[1,1,128,256]{3,2,1,0:T(8,128)(2,1)S(1)} %get-tuple-element.19), channel_id=1, source_target_pairs={{1,0},{2,1},{3,2},{4,3},{5,4},{6,5},{7,6},{9,8},{10,9},{11,10},{12... | collective-permute-start | bytes 196616 | tf_op jit(solution)/shard_map/ppermute | solution.py:15
  7.9 0.6 collective-permute-done
  8.4 4.3 %collective-permute-done.1 = bf16[1,1,128,256]{3,2,1,0:T(8,128)(2,1)S(1)} collective-permute-done((bf16[1,1,128,256]{3,2,1,0:T(8,128)(2,1)S(1)}, bf16[1,1,128,256]{3,2,1,0:T(8,128)(2,1)S(1)}, u32[]{:S(2)}, u32[]{:S(2)}) %collective-permute-start.1) | collective-permute-done | bytes 65568 | tf_op jit(solution)/shard_map/ppermute | solution.py:15
  12.7 0.1 pad_maximum_fusion.3
  12.8 3.5 %collective-permute-start.2 = (bf16[1,10,128,256]{3,2,1,0:T(8,128)(2,1)S(1)}, bf16[1,10,128,256]{3,2,1,0:T(8,128)(2,1)S(1)}, u32[]{:S(2)}, u32[]{:S(2)}) collective-permute-start(bf16[1,10,128,256]{3,2,1,0:T(8,128)(2,1)S(1)} %pad_maximum_fusion.3), channel_id=1, source_target_pairs={{0,16},{8,24},{16,32},{24,40},{32,48},{40,56},{48,64},{56,72},{64,... | collective-permute-start | bytes 1966088 | tf_op jit(solution)/shard_map/ppermute | solution.py:23
  16.3 1.9 %collective-permute-start.3 = (bf16[1,10,128,256]{3,2,1,0:T(8,128)(2,1)S(1)}, bf16[1,10,128,256]{3,2,1,0:T(8,128)(2,1)S(1)}, u32[]{:S(2)}, u32[]{:S(2)}) collective-permute-start(bf16[1,10,128,256]{3,2,1,0:T(8,128)(2,1)S(1)} %pad_maximum_fusion.3), channel_id=1, source_target_pairs={{0,8},{8,16},{16,24},{24,32},{32,40},{40,48},{48,56},{56,64},{64,7... | collective-permute-start | bytes 1966088 | tf_op jit(solution)/shard_map/ppermute | solution.py:23
  18.2 16.3 %collective-permute-done.2 = bf16[1,10,128,256]{3,2,1,0:T(8,128)(2,1)S(1)} collective-permute-done((bf16[1,10,128,256]{3,2,1,0:T(8,128)(2,1)S(1)}, bf16[1,10,128,256]{3,2,1,0:T(8,128)(2,1)S(1)}, u32[]{:S(2)}, u32[]{:S(2)}) %collective-permute-start.2) | collective-permute-done | bytes 655392 | tf_op jit(solution)/shard_map/ppermute | solution.py:23
  34.5 4.6 %collective-permute-done.3 = bf16[1,10,128,256]{3,2,1,0:T(8,128)(2,1)S(1)} collective-permute-done((bf16[1,10,128,256]{3,2,1,0:T(8,128)(2,1)S(1)}, bf16[1,10,128,256]{3,2,1,0:T(8,128)(2,1)S(1)}, u32[]{:S(2)}, u32[]{:S(2)}) %collective-permute-start.3) | collective-permute-done | bytes 655392 | tf_op jit(solution)/shard_map/ppermute | solution.py:23
  39.1 0.9 fusion.14
  40.0 1.4 %fusion.64 = (bf16[3,10,128,256]{3,2,1,0:T(8,128)(2,1)S(1)}, bf16[3,10,128,256]{3,2,1,0:T(8,128)(2,1)S(1)}) fusion(bf16[3,10,130,256]{3,2,1,0:T(8,128)(2,1)S(1)} %fusion.14), kind=kLoop, calls=%fused_computation.124 | loop fusion | bytes 7864320 | tf_op jit(solution)/shard_map/slice | solution.py:49
  41.4 0.0 copy-start.3
  41.4 0.7 pad_maximum_fusion.1
  42.1 1.3 %copy-done.3 = bf16[3,3,3,256,256]{4,3,2,1,0:T(8,128)(2,1)S(1)} copy-done((bf16[3,3,3,256,256]{4,3,2,1,0:T(8,128)(2,1)S(1)}, bf16[3,3,3,256,256]{4,3,2,1,0:T(8,128)(2,1)}, u32[]{:S(2)}) %copy-start.3) | copy-done | bytes 3538968
  43.4 0.6 fusion.26
  44.0 0.6 fusion.27
  44.6 0.6 fusion.28
  45.2 0.6 fusion.29
  45.8 0.6 fusion.30
  46.4 0.6 fusion.31
  47.0 0.6 fusion.32
  47.5 0.6 fusion.33
  48.1 0.0 copy-start.4
  48.1 1.0 multiply_reduce_fusion
  49.1 0.4 fusion.62
  49.5 3.8 %collective-permute-start.4 = (bf16[1,1,128,256]{3,2,1,0:T(8,128)(2,1)S(1)}, bf16[1,1,128,256]{3,2,1,0:T(8,128)(2,1)S(1)}, u32[]{:S(2)}, u32[]{:S(2)}) collective-permute-start(bf16[1,1,128,256]{3,2,1,0:T(8,128)(2,1)S(1)} %get-tuple-element.16), channel_id=1, source_target_pairs={{0,1},{1,2},{2,3},{3,4},{4,5},{5,6},{6,7},{8,9},{9,10},{10,11},{11... | collective-permute-start | bytes 196616 | tf_op jit(solution)/shard_map/ppermute | solution.py:14
  53.4 1.3 %collective-permute-start.5 = (bf16[1,1,128,256]{3,2,1,0:T(8,128)(2,1)S(1)}, bf16[1,1,128,256]{3,2,1,0:T(8,128)(2,1)S(1)}, u32[]{:S(2)}, u32[]{:S(2)}) collective-permute-start(bf16[1,1,128,256]{3,2,1,0:T(8,128)(2,1)S(1)} %get-tuple-element.17), channel_id=1, source_target_pairs={{1,0},{2,1},{3,2},{4,3},{5,4},{6,5},{7,6},{9,8},{10,9},{11,10},{12... | collective-permute-start | bytes 196616 | tf_op jit(solution)/shard_map/ppermute | solution.py:15
  54.7 0.6 collective-permute-done.4
  55.2 5.4 %collective-permute-done.5 = bf16[1,1,128,256]{3,2,1,0:T(8,128)(2,1)S(1)} collective-permute-done((bf16[1,1,128,256]{3,2,1,0:T(8,128)(2,1)S(1)}, bf16[1,1,128,256]{3,2,1,0:T(8,128)(2,1)S(1)}, u32[]{:S(2)}, u32[]{:S(2)}) %collective-permute-start.5) | collective-permute-done | bytes 65568 | tf_op jit(solution)/shard_map/ppermute | solution.py:15
  60.6 0.1 pad_maximum_fusion.4
  60.7 1.9 %collective-permute-start.6 = (bf16[1,10,128,256]{3,2,1,0:T(8,128)(2,1)S(1)}, bf16[1,10,128,256]{3,2,1,0:T(8,128)(2,1)S(1)}, u32[]{:S(2)}, u32[]{:S(2)}) collective-permute-start(bf16[1,10,128,256]{3,2,1,0:T(8,128)(2,1)S(1)} %pad_maximum_fusion.4), channel_id=1, source_target_pairs={{0,16},{8,24},{16,32},{24,40},{32,48},{40,56},{48,64},{56,72},{64,... | collective-permute-start | bytes 1966088 | tf_op jit(solution)/shard_map/ppermute | solution.py:23
  62.6 2.1 %collective-permute-start.7 = (bf16[1,10,128,256]{3,2,1,0:T(8,128)(2,1)S(1)}, bf16[1,10,128,256]{3,2,1,0:T(8,128)(2,1)S(1)}, u32[]{:S(2)}, u32[]{:S(2)}) collective-permute-start(bf16[1,10,128,256]{3,2,1,0:T(8,128)(2,1)S(1)} %pad_maximum_fusion.4), channel_id=1, source_target_pairs={{0,8},{8,16},{16,24},{24,32},{32,40},{40,48},{48,56},{56,64},{64,7... | collective-permute-start | bytes 1966088 | tf_op jit(solution)/shard_map/ppermute | solution.py:23
  64.8 17.6 %collective-permute-done.6 = bf16[1,10,128,256]{3,2,1,0:T(8,128)(2,1)S(1)} collective-permute-done((bf16[1,10,128,256]{3,2,1,0:T(8,128)(2,1)S(1)}, bf16[1,10,128,256]{3,2,1,0:T(8,128)(2,1)S(1)}, u32[]{:S(2)}, u32[]{:S(2)}) %collective-permute-start.6) | collective-permute-done | bytes 655392 | tf_op jit(solution)/shard_map/ppermute | solution.py:23
  82.4 2.0 %collective-permute-done.7 = bf16[1,10,128,256]{3,2,1,0:T(8,128)(2,1)S(1)} collective-permute-done((bf16[1,10,128,256]{3,2,1,0:T(8,128)(2,1)S(1)}, bf16[1,10,128,256]{3,2,1,0:T(8,128)(2,1)S(1)}, u32[]{:S(2)}, u32[]{:S(2)}) %collective-permute-start.7) | collective-permute-done | bytes 655392 | tf_op jit(solution)/shard_map/ppermute | solution.py:23
  84.4 0.9 fusion.4
  85.3 1.4 %fusion.63 = (bf16[3,10,128,256]{3,2,1,0:T(8,128)(2,1)S(1)}, bf16[3,10,128,256]{3,2,1,0:T(8,128)(2,1)S(1)}) fusion(bf16[3,10,130,256]{3,2,1,0:T(8,128)(2,1)S(1)} %fusion.4), kind=kLoop, calls=%fused_computation.123 | loop fusion | bytes 7864320 | tf_op jit(solution)/shard_map/slice | solution.py:49
  86.7 0.0 copy-start.2
  86.7 0.7 pad_maximum_fusion.2
  87.4 1.3 %copy-done.2 = bf16[3,3,3,256,256]{4,3,2,1,0:T(8,128)(2,1)S(1)} copy-done((bf16[3,3,3,256,256]{4,3,2,1,0:T(8,128)(2,1)S(1)}, bf16[3,3,3,256,256]{4,3,2,1,0:T(8,128)(2,1)}, u32[]{:S(2)}) %copy-start.2) | copy-done | bytes 3538968
  88.7 0.6 fusion.17
  89.3 0.6 fusion.18
  89.9 0.6 fusion.19
  90.5 0.6 fusion.20
  91.0 0.6 fusion.21
  91.6 0.6 fusion.22
  92.2 0.6 fusion.23
  92.8 0.6 fusion.24
  93.4 1.1 fusion.53
  94.5 4.8 %collective-permute-start.8 = (bf16[1,1,128,256]{3,2,1,0:T(8,128)(2,1)S(1)}, bf16[1,1,128,256]{3,2,1,0:T(8,128)(2,1)S(1)}, u32[]{:S(2)}, u32[]{:S(2)}) collective-permute-start(bf16[1,1,128,256]{3,2,1,0:T(8,128)(2,1)S(1)} %get-tuple-element.14), channel_id=1, source_target_pairs={{0,1},{1,2},{2,3},{3,4},{4,5},{5,6},{6,7},{8,9},{9,10},{10,11},{11... | collective-permute-start | bytes 196616 | tf_op jit(solution)/shard_map/ppermute | solution.py:14
  99.4 1.5 %collective-permute-start.9 = (bf16[1,1,128,256]{3,2,1,0:T(8,128)(2,1)S(1)}, bf16[1,1,128,256]{3,2,1,0:T(8,128)(2,1)S(1)}, u32[]{:S(2)}, u32[]{:S(2)}) collective-permute-start(bf16[1,1,128,256]{3,2,1,0:T(8,128)(2,1)S(1)} %get-tuple-element.15), channel_id=1, source_target_pairs={{1,0},{2,1},{3,2},{4,3},{5,4},{6,5},{7,6},{9,8},{10,9},{11,10},{12... | collective-permute-start | bytes 196616 | tf_op jit(solution)/shard_map/ppermute | solution.py:15
  101.0 0.3 collective-permute-done.8
  101.3 4.3 %collective-permute-done.9 = bf16[1,1,128,256]{3,2,1,0:T(8,128)(2,1)S(1)} collective-permute-done((bf16[1,1,128,256]{3,2,1,0:T(8,128)(2,1)S(1)}, bf16[1,1,128,256]{3,2,1,0:T(8,128)(2,1)S(1)}, u32[]{:S(2)}, u32[]{:S(2)}) %collective-permute-start.9) | collective-permute-done | bytes 65568 | tf_op jit(solution)/shard_map/ppermute | solution.py:15
  105.5 0.1 maximum_bitcast_fusion
  105.6 0.1 broadcast_in_dim.14
  105.8 0.1 slice_bitcast_fusion.84
  105.9 3.1 %broadcast_in_dim.16 = bf16[18,128,2,256]{3,2,1,0:T(2,128)(2,1)} broadcast(bf16[18,128,256]{2,1,0:T(8,128)(2,1)S(1)} %slice_bitcast_fusion.84), dimensions={0,1,3} | broadcast | bytes 3538944 | tf_op jit(solution)/shard_map/broadcast_in_dim | solution.py:81
  109.0 5.0 %broadcast_in_dim.17 = bf16[1,18,256,256]{3,2,1,0:T(8,128)(2,1)S(1)} reshape(bf16[18,128,2,256]{3,2,1,0:T(2,128)(2,1)} %broadcast_in_dim.16) | data formatting | bytes 4718592 | tf_op jit(solution)/shard_map/broadcast_in_dim | solution.py:81
  114.0 1.2 pad_slice_fusion.1
  115.2 0.6 pad_maximum_fusion
  115.8 1.8 %fusion.1 = f32[16,256,128]{2,1,0:T(8,128)S(1)} fusion(bf16[768,128,1]{1,0,2:T(8,128)(2,1)S(1)} %bitcast.231, bf16[1,18,256,768]{3,2,1,0:T(8,128)(2,1)S(1)} %pad_maximum_fusion), kind=kOutput, calls=%fused_computation.4 | convolution fusion | flops 805306368 | bytes 8585216 | tf_op jit(solution)/shard_map/frwc,co->frwo/dot_general | solution.py:87
  117.6 1.8 %fusion = f32[16,256,128]{2,1,0:T(8,128)S(1)} fusion(bf16[768,128,1]{1,0,2:T(8,128)(2,1)S(1)} %bitcast.230, bf16[1,18,256,768]{3,2,1,0:T(8,128)(2,1)S(1)} %pad_maximum_fusion), kind=kOutput, calls=%fused_computation.2 | convolution fusion | flops 805306368 | bytes 8585216 | tf_op jit(solution)/shard_map/frwc,co->frwo/dot_general | solution.py:87
  119.4 2.8 %fusion.47 = bf16[1,16,256,128]{3,2,1,0:T(8,128)(2,1)} fusion(f32[16,256,128]{2,1,0:T(8,128)S(1)} %fusion, f32[16,256,128]{2,1,0:T(8,128)S(1)} %fusion.1, bf16[768,128,1]{1,0,2:T(8,128)(2,1)S(1)} %bitcast.229, bf16[1,18,256,768]{3,2,1,0:T(8,128)(2,1)S(1)} %pad_maximum_fusion), kind=kOutput, calls=%fused_computation.81 | convolution fusion | flops 806879232 | bytes 11730944 | tf_op jit(solution)/shard_map/frwc,co->frwo/dot_general | solution.py:87
  (11 shorter events, 0.1 us)
Async XLA Ops:
  2.7 5.7 %collective-permute-start = (bf16[1,1,128,256]{3,2,1,0:T(8,128)(2,1)S(1)}, bf16[1,1,128,256]{3,2,1,0:T(8,128)(2,1)S(1)}, u32[]{:S(2)}, u32[]{:S(2)}) collective-permute-start(bf16[1,1,128,256]{3,2,1,0:T(8,128)(2,1)S(1)} %get-tuple-element.18), channel_id=1, source_target_pairs={{0,1},{1,2},{2,3},{3,4},{4,5},{5,6},{6,7},{8,9},{9,10},{10,11},{11... | collective-permute-start | bytes 196616 | tf_op jit(solution)/shard_map/ppermute | solution.py:14
  6.6 6.2 %collective-permute-start.1 = (bf16[1,1,128,256]{3,2,1,0:T(8,128)(2,1)S(1)}, bf16[1,1,128,256]{3,2,1,0:T(8,128)(2,1)S(1)}, u32[]{:S(2)}, u32[]{:S(2)}) collective-permute-start(bf16[1,1,128,256]{3,2,1,0:T(8,128)(2,1)S(1)} %get-tuple-element.19), channel_id=1, source_target_pairs={{1,0},{2,1},{3,2},{4,3},{5,4},{6,5},{7,6},{9,8},{10,9},{11,10},{12... | collective-permute-start | bytes 196616 | tf_op jit(solution)/shard_map/ppermute | solution.py:15
  12.8 21.7 %collective-permute-start.2 = (bf16[1,10,128,256]{3,2,1,0:T(8,128)(2,1)S(1)}, bf16[1,10,128,256]{3,2,1,0:T(8,128)(2,1)S(1)}, u32[]{:S(2)}, u32[]{:S(2)}) collective-permute-start(bf16[1,10,128,256]{3,2,1,0:T(8,128)(2,1)S(1)} %pad_maximum_fusion.3), channel_id=1, source_target_pairs={{0,16},{8,24},{16,32},{24,40},{32,48},{40,56},{48,64},{56,72},{64,... | collective-permute-start | bytes 1966088 | tf_op jit(solution)/shard_map/ppermute | solution.py:23
  16.3 22.8 %collective-permute-start.3 = (bf16[1,10,128,256]{3,2,1,0:T(8,128)(2,1)S(1)}, bf16[1,10,128,256]{3,2,1,0:T(8,128)(2,1)S(1)}, u32[]{:S(2)}, u32[]{:S(2)}) collective-permute-start(bf16[1,10,128,256]{3,2,1,0:T(8,128)(2,1)S(1)} %pad_maximum_fusion.3), channel_id=1, source_target_pairs={{0,8},{8,16},{16,24},{24,32},{32,40},{40,48},{48,56},{56,64},{64,7... | collective-permute-start | bytes 1966088 | tf_op jit(solution)/shard_map/ppermute | solution.py:23
  41.4 2.0 %copy-start.3 = (bf16[3,3,3,256,256]{4,3,2,1,0:T(8,128)(2,1)S(1)}, bf16[3,3,3,256,256]{4,3,2,1,0:T(8,128)(2,1)}, u32[]{:S(2)}) copy-start(bf16[3,3,3,256,256]{4,3,2,1,0:T(8,128)(2,1)} %param.8) | copy-start | bytes 10616836
  48.1 1.0 copy-start.4
  49.5 5.7 %collective-permute-start.4 = (bf16[1,1,128,256]{3,2,1,0:T(8,128)(2,1)S(1)}, bf16[1,1,128,256]{3,2,1,0:T(8,128)(2,1)S(1)}, u32[]{:S(2)}, u32[]{:S(2)}) collective-permute-start(bf16[1,1,128,256]{3,2,1,0:T(8,128)(2,1)S(1)} %get-tuple-element.16), channel_id=1, source_target_pairs={{0,1},{1,2},{2,3},{3,4},{4,5},{5,6},{6,7},{8,9},{9,10},{10,11},{11... | collective-permute-start | bytes 196616 | tf_op jit(solution)/shard_map/ppermute | solution.py:14
  53.4 7.3 %collective-permute-start.5 = (bf16[1,1,128,256]{3,2,1,0:T(8,128)(2,1)S(1)}, bf16[1,1,128,256]{3,2,1,0:T(8,128)(2,1)S(1)}, u32[]{:S(2)}, u32[]{:S(2)}) collective-permute-start(bf16[1,1,128,256]{3,2,1,0:T(8,128)(2,1)S(1)} %get-tuple-element.17), channel_id=1, source_target_pairs={{1,0},{2,1},{3,2},{4,3},{5,4},{6,5},{7,6},{9,8},{10,9},{11,10},{12... | collective-permute-start | bytes 196616 | tf_op jit(solution)/shard_map/ppermute | solution.py:15
  60.7 21.7 %collective-permute-start.6 = (bf16[1,10,128,256]{3,2,1,0:T(8,128)(2,1)S(1)}, bf16[1,10,128,256]{3,2,1,0:T(8,128)(2,1)S(1)}, u32[]{:S(2)}, u32[]{:S(2)}) collective-permute-start(bf16[1,10,128,256]{3,2,1,0:T(8,128)(2,1)S(1)} %pad_maximum_fusion.4), channel_id=1, source_target_pairs={{0,16},{8,24},{16,32},{24,40},{32,48},{40,56},{48,64},{56,72},{64,... | collective-permute-start | bytes 1966088 | tf_op jit(solution)/shard_map/ppermute | solution.py:23
  62.6 21.7 %collective-permute-start.7 = (bf16[1,10,128,256]{3,2,1,0:T(8,128)(2,1)S(1)}, bf16[1,10,128,256]{3,2,1,0:T(8,128)(2,1)S(1)}, u32[]{:S(2)}, u32[]{:S(2)}) collective-permute-start(bf16[1,10,128,256]{3,2,1,0:T(8,128)(2,1)S(1)} %pad_maximum_fusion.4), channel_id=1, source_target_pairs={{0,8},{8,16},{16,24},{24,32},{32,40},{40,48},{48,56},{56,64},{64,7... | collective-permute-start | bytes 1966088 | tf_op jit(solution)/shard_map/ppermute | solution.py:23
  86.7 2.0 %copy-start.2 = (bf16[3,3,3,256,256]{4,3,2,1,0:T(8,128)(2,1)S(1)}, bf16[3,3,3,256,256]{4,3,2,1,0:T(8,128)(2,1)}, u32[]{:S(2)}) copy-start(bf16[3,3,3,256,256]{4,3,2,1,0:T(8,128)(2,1)} %param.10) | copy-start | bytes 10616836
  92.2 1.2 copy-start
  93.4 7.5 %copy-start.1 = (bf16[3,3,256,128]{3,2,1,0:T(8,128)(2,1)S(1)}, bf16[3,3,256,128]{3,2,1,0:T(8,128)(2,1)}, u32[]{:S(2)}) copy-start(bf16[3,3,256,128]{3,2,1,0:T(8,128)(2,1)} %param.11) | copy-start | bytes 1769476
  94.5 6.7 %collective-permute-start.8 = (bf16[1,1,128,256]{3,2,1,0:T(8,128)(2,1)S(1)}, bf16[1,1,128,256]{3,2,1,0:T(8,128)(2,1)S(1)}, u32[]{:S(2)}, u32[]{:S(2)}) collective-permute-start(bf16[1,1,128,256]{3,2,1,0:T(8,128)(2,1)S(1)} %get-tuple-element.14), channel_id=1, source_target_pairs={{0,1},{1,2},{2,3},{3,4},{4,5},{5,6},{6,7},{8,9},{9,10},{10,11},{11... | collective-permute-start | bytes 196616 | tf_op jit(solution)/shard_map/ppermute | solution.py:14
  99.4 6.2 %collective-permute-start.9 = (bf16[1,1,128,256]{3,2,1,0:T(8,128)(2,1)S(1)}, bf16[1,1,128,256]{3,2,1,0:T(8,128)(2,1)S(1)}, u32[]{:S(2)}, u32[]{:S(2)}) collective-permute-start(bf16[1,1,128,256]{3,2,1,0:T(8,128)(2,1)S(1)} %get-tuple-element.15), channel_id=1, source_target_pairs={{1,0},{2,1},{3,2},{4,3},{5,4},{6,5},{7,6},{9,8},{10,9},{11,10},{12... | collective-permute-start | bytes 196616 | tf_op jit(solution)/shard_map/ppermute | solution.py:15
where the time goes:
time: 123 us; the launch traced here: 122 us
  waiting for transfers between devices  55.8 us (45%)
  starting transfers between devices  26 us (21%)
  matrix products  17.8 us (14%)
  local copies, waits for them, and re-layouts  15.1 us (12%)
  other arithmetic  7.1 us (6%)
    ppermute x4, waiting for transfers between devices, from_behind(): return lax.ppermute(block, axis, route)  40.4 us
    ppermute x3, waiting for transfers between devices, with_halo(): after = lax.ppermute(leading, axis, down)  13.9 us
    ppermute x3, starting transfers between devices, with_halo(): before = lax.ppermute(last, axis, up)  12.5 us
    dot_general x18, matrix products, causal(): jnp.einsum('frwc,co->frwo', window, matrices[depth_tap, row_tap], preferr...  11.4 us
    ppermute x4, starting transfers between devices, from_behind(): return lax.ppermute(block, axis, route)  9.43 us
    broadcast_in_dim x2, local copies, waits for them, and re-layouts, body(): grown = jnp.repeat(grown, 2, axis=2)  8.16 us
    dot_general x3, matrix products, body(): jnp.einsum('frwc,co->frwo', window, matrices[row_tap], preferred_element_...  6.44 us
    ppermute x3, starting transfers between devices, with_halo(): after = lax.ppermute(leading, axis, down)  4.1 us
  transfers between devices with their start and end apart: 10, of which 10 were waited for; matrix products, arithmetic and copies ran while one was open for 0% of the time, Pallas kernels for 0%

commit v1 on v0

v1 whole, which is shorter than its diff:
```python
import functools

import jax
import jax.numpy as jnp
from jax import lax
from jax.experimental import pallas as pl
from jax.experimental.pallas import tpu as pltpu
from jax.sharding import PartitionSpec as P

MESH = pl.DeviceIdType.MESH
PAD = 8


def windows(width, first, step):
    edges = [0, first]
    while edges[-1] < width:
        edges.append(min(edges[-1] + step, width))
    return list(zip(edges[:-1], edges[1:]))


def settled(wins, width, lag):
    edges = [0] + [max(hi - lag, 0) for _, hi in wins[:-1]] + [width]
    return list(zip(edges[:-1], edges[1:]))


def norm_silu(values, scales):
    mean_sq = jnp.mean(values * values, axis=-1, keepdims=True)
    u = values * lax.rsqrt(mean_sq + 1e-06) * scales
    return 0.5 * u * (1.0 + jnp.tanh(0.5 * u))


def kernel(
    sizes,
    wins,
    latent,
    gain_one,
    gain_two,
    conv_one,
    conv_two,
    up_weight,
    out,
    lat,
    weights,
    up_raw,
    up_mat,
    held,
    block,
    sums,
    up_sums,
    woven,
    packed,
    load_sem,
    out_sem,
    frame_send,
    frame_recv,
    pair_send,
    pair_recv,
    rim_send,
    rim_recv,
    edge_send,
    edge_recv,
):
    frames, bands = sizes
    height, width, channels = lat.shape
    growth = up_raw.shape[3]
    tm, rw = lax.axis_index("tm"), lax.axis_index("rows")
    odd = lax.rem(tm, 2)
    mate = (tm + 1 - 2 * odd, rw)
    ahead = (lax.rem(tm + 2, frames), rw)
    behind = (lax.rem(tm + frames - 2, frames), rw)
    above = (tm, lax.rem(rw + bands - 1, bands))
    below = (tm, lax.rem(rw + 1, bands))
    body = pl.ds(1, height)

    loads = [pltpu.make_async_copy(latent.at[0], lat, load_sem.at[0])]
    for stage, conv in enumerate((conv_one, conv_two)):
        for e in range(3):
            loads.append(
                pltpu.make_async_copy(
                    conv.at[:, :, e], weights.at[stage, e], load_sem.at[1 + 3 * stage + e]
                )
            )
    loads.append(pltpu.make_async_copy(up_weight, up_raw, load_sem.at[7]))
    for load in loads:
        load.start()

    barrier = pltpu.get_barrier_semaphore()
    for peer in (behind, mate, above, below):
        pl.semaphore_signal(barrier, inc=1, device_id=peer, device_id_type=MESH)

    def remote(src, dst, send, recv, peer):
        return pltpu.make_async_remote_copy(
            src_ref=src, dst_ref=dst, send_sem=send, recv_sem=recv, device_id=peer, device_id_type=MESH
        )

    def to_ahead(s, c):
        cols = pl.ds(wins[s][c][0], wins[s][c][1] - wins[s][c][0])
        return remote(
            held.at[s, 2, body, cols],
            held.at[s, 0, body, cols],
            frame_send.at[s, c],
            frame_recv.at[s, c],
            ahead,
        )

    def to_mate(s, c):
        cols = pl.ds(wins[s][c][0], wins[s][c][1] - wins[s][c][0])
        return remote(
            held.at[s, 2 - 2 * odd, body, cols],
            held.at[s, 1, body, cols],
            pair_send.at[s, c],
            pair_recv.at[s, c],
            mate,
        )

    def to_rims(s, c):
        cols = pl.ds(wins[s][c][0], wins[s][c][1] - wins[s][c][0])
        return [
            remote(
                held.at[s, :, mine, cols],
                held.at[s, :, theirs, cols],
                rim_send.at[s, c, k],
                rim_recv.at[s, c, k],
                peer,
            )
            for k, (mine, theirs, peer) in enumerate(((1, height + 1, above), (height, 0, below)))
        ]

    def to_edges(c):
        cols = pl.ds(wins[2][c][0], wins[2][c][1] - wins[2][c][0])
        return [
            remote(
                block.at[mine, cols],
                block.at[theirs, cols],
                edge_send.at[c, k],
                edge_recv.at[c, k],
                peer,
            )
            for k, (mine, theirs, peer) in enumerate(((1, height + 1, above), (height, 0, below)))
        ]

    def take_frame(s, c):
        lo, hi = wins[s][c]
        to_ahead(s, c).wait_recv()

        @pl.when(tm < 2)
        def _():
            held[s, 0, 1 : height + 1, lo:hi] = jnp.zeros((height, hi - lo, channels), held.dtype)

        to_mate(s, c).start()

    def take_pair(s, c):
        to_mate(s, c).wait_recv()
        for copy in to_rims(s, c):
            copy.start()

    def take_rims(s, c):
        lo, hi = wins[s][c]
        for copy in to_rims(s, c):
            copy.wait_recv()
        blank = jnp.zeros((3, hi - lo, channels), held.dtype)

        @pl.when(rw == 0)
        def _():
            held[s, :, 0, lo:hi] = blank

        @pl.when(rw == bands - 1)
        def _():
            held[s, :, height + 1, lo:hi] = blank

    def multiply(s, c):
        lo, hi = wins[s][c]
        rows = height * (hi - lo)
        left = jnp.concatenate(
            [
                held[s, a, b : b + height, lo:hi].reshape(rows, channels)
                for a in range(3)
                for b in range(3)
            ],
            axis=1,
        )
        for e in range(3):
            term = jnp.dot(
                left,
                weights[s, e].reshape(9 * channels, channels),
                preferred_element_type=jnp.float32,
            )
            sums[e, :, PAD + lo : PAD + hi] = term.reshape(height, hi - lo, channels)

    def total(r, lo, hi):
        return (
            sums[0, r, PAD + lo - 1 : PAD + hi - 1]
            + sums[1, r, PAD + lo : PAD + hi]
            + sums[2, r, PAD + lo + 1 : PAD + hi + 1]
        )

    def settle_one(c):
        lo, hi = wins[1][c]

        def row(r, _):
            held[1, 2, 1 + r, lo:hi] = norm_silu(total(r, lo, hi), gain_two[...]).astype(held.dtype)
            return 0

        lax.fori_loop(0, height, row, 0)
        to_ahead(1, c).start()

    def settle_two(c):
        lo, hi = wins[2][c]

        def row(r, _):
            value = lat[r, lo:hi].astype(jnp.float32) + total(r, lo, hi)
            block[1 + r, lo:hi] = value.astype(block.dtype)
            return 0

        lax.fori_loop(0, height, row, 0)
        for copy in to_edges(c):
            copy.start()

    def upsample(c):
        lo, hi = wins[2][c]
        for copy in to_edges(c):
            copy.wait_recv()
        blank = jnp.zeros((hi - lo, channels), block.dtype)

        @pl.when(rw == 0)
        def _():
            block[0, lo:hi] = blank

        @pl.when(rw == bands - 1)
        def _():
            block[height + 1, lo:hi] = blank

        rows = height * (hi - lo)
        for p in range(2):
            left = jnp.concatenate(
                [block[p + d : p + d + height, lo:hi].reshape(rows, channels) for d in range(2)], axis=1
            )
            term = jnp.dot(left, up_mat[p], preferred_element_type=jnp.float32)
            up_sums[p, :, PAD + lo : PAD + hi] = term.reshape(height, hi - lo, 4 * growth)

    def weave(c):
        lo, hi = wins[3][c]
        n = hi - lo
        if n == 0:
            return
        g = growth

        def row(r, _):
            for p in range(2):
                even = (
                    up_sums[p, r, PAD + lo - 1 : PAD + hi - 1, 0:g]
                    + up_sums[p, r, PAD + lo : PAD + hi, g : 2 * g]
                )
                odds = (
                    up_sums[p, r, PAD + lo : PAD + hi, 2 * g : 3 * g]
                    + up_sums[p, r, PAD + lo + 1 : PAD + hi + 1, 3 * g : 4 * g]
                )
                woven[pl.ds(0, n, stride=2), :] = even
                woven[pl.ds(1, n, stride=2), :] = odds
                packed[2 * r + p, 2 * lo : 2 * hi] = woven[0 : 2 * n, :].astype(packed.dtype)
            return 0

        lax.fori_loop(0, height, row, 0)
        to_out(c).start()

    def to_out(c):
        lo, hi = wins[3][c]
        cols = pl.ds(2 * lo, 2 * (hi - lo))
        return pltpu.make_async_copy(packed.at[:, cols], out.at[0, :, cols], out_sem.at[c])

    loads[0].wait()
    pl.semaphore_wait(barrier, 4)
    for c, (lo, hi) in enumerate(wins[0]):

        def row(r, _, lo=lo, hi=hi):
            value = lat[r, lo:hi].astype(jnp.float32)
            held[0, 2, 1 + r, lo:hi] = norm_silu(value, gain_one[...]).astype(held.dtype)
            return 0

        lax.fori_loop(0, height, row, 0)
        to_ahead(0, c).start()

    sums[0, :, 0:PAD] = jnp.zeros((height, PAD, channels), jnp.float32)
    sums[2, :, PAD + width :] = jnp.zeros((height, PAD, channels), jnp.float32)
    for p in range(2):
        up_sums[p, :, 0:PAD, 0:growth] = jnp.zeros((height, PAD, growth), jnp.float32)
        up_sums[p, :, PAD + width :, 3 * growth :] = jnp.zeros((height, PAD, growth), jnp.float32)
    loads[7].wait()
    for p, groups in enumerate((((0,), (1, 2)), ((0, 1), (2,)))):
        for d, group in enumerate(groups):
            col = [sum(up_raw[b, e].astype(jnp.float32) for b in group) for e in range(3)]
            parts = (col[0], col[1] + col[2], col[0] + col[1], col[2])
            for k, part in enumerate(parts):
                up_mat[p, d * channels : (d + 1) * channels, k * growth : (k + 1) * growth] = part.astype(
                    up_mat.dtype
                )

    count = len(wins[0])
    take_frame(0, 0)
    take_pair(0, 0)
    for load in loads[1:4]:
        load.wait()
    for c in range(count):
        if c + 1 < count:
            take_frame(0, c + 1)
        take_rims(0, c)
        multiply(0, c)
        settle_one(c)
        if c + 1 < count:
            take_pair(0, c + 1)

    count = len(wins[1])
    take_frame(1, 0)
    take_pair(1, 0)
    for load in loads[4:7]:
        load.wait()
    for c in range(count):
        if c + 1 < count:
            take_frame(1, c + 1)
        take_rims(1, c)
        multiply(1, c)
        settle_two(c)
        if c + 1 < count:
            take_pair(1, c + 1)
        if c > 0:
            upsample(c - 1)
            weave(c - 1)
    upsample(count - 1)
    weave(count - 1)

    for s in range(2):
        for c in range(len(wins[s])):
            to_ahead(s, c).wait_send()
            to_mate(s, c).wait_send()
            for copy in to_rims(s, c):
                copy.wait_send()
    for c in range(len(wins[2])):
        for copy in to_edges(c):
            copy.wait_send()
    for c in range(len(wins[3])):
        if wins[3][c][1] > wins[3][c][0]:
            to_out(c).wait()


def fused(sizes, latent, gain_one, conv_one, gain_two, conv_two, up_weight):
    _, height, width, channels = latent.shape
    growth = up_weight.shape[3]
    first = windows(width, 48, 32)
    second = settled(first, width, 16)
    third = settled(second, width, 16)
    fourth = settled(third, width, 8)
    wins = (first, second, third, fourth)
    count = len(first)
    dma = pltpu.SemaphoreType.DMA
    bf16, f32 = jnp.bfloat16, jnp.float32
    return pl.pallas_call(
        functools.partial(kernel, sizes, wins),
        out_shape=jax.ShapeDtypeStruct((1, 2 * height, 2 * width, growth), bf16),
        in_specs=[
            pl.BlockSpec(memory_space=pl.ANY),
            pl.BlockSpec(memory_space=pltpu.VMEM),
            pl.BlockSpec(memory_space=pltpu.VMEM),
            pl.BlockSpec(memory_space=pl.ANY),
            pl.BlockSpec(memory_space=pl.ANY),
            pl.BlockSpec(memory_space=pl.ANY),
        ],
        out_specs=pl.BlockSpec(memory_space=pl.ANY),
        scratch_shapes=[
            pltpu.VMEM((height, width, channels), bf16),
            pltpu.VMEM((2, 3, 3, 3, channels, channels), bf16),
            pltpu.VMEM((3, 3, channels, growth), bf16),
            pltpu.VMEM((2, 2 * channels, 4 * growth), bf16),
            pltpu.VMEM((2, 3, height + 2, width, channels), bf16),
            pltpu.VMEM((height + 2, width, channels), bf16),
            pltpu.VMEM((3, height, width + 2 * PAD, channels), f32),
            pltpu.VMEM((2, height, width + 2 * PAD, 4 * growth), f32),
            pltpu.VMEM((2 * width, growth), f32),
            pltpu.VMEM((2 * height, 2 * width, growth), bf16),
            dma((8,)),
            dma((count,)),
            dma((2, count)),
            dma((2, count)),
            dma((2, count)),
            dma((2, count)),
            dma((2, count, 2)),
            dma((2, count, 2)),
            dma((count, 2)),
            dma((count, 2)),
        ],
        compiler_params=pltpu.CompilerParams(
            collective_id=0, has_side_effects=True, vmem_limit_bytes=56 * 1024 * 1024
        ),
    )(
        latent,
        gain_one.reshape(1, channels),
        gain_two.reshape(1, channels),
        conv_one,
        conv_two,
        up_weight,
    )


def solution(mesh):
    sizes = (mesh.shape["tm"], mesh.shape["rows"])
    placed = (P("tm", "rows", None, None), P(), P(), P(), P(), P())
    return jax.shard_map(
        functools.partial(fused, sizes),
        mesh=mesh,
        in_specs=placed,
        out_specs=P("tm", "rows", None, None),
        check_vma=False,
    )
```

time: 123 us -> 71.4 us (0.58)
  Pallas kernels: 0 us -> 68.1 us
  waiting for transfers between devices: 55.8 us -> 0 us
  starting transfers between devices: 26 us -> 0 us
  matrix products: 17.8 us -> 0 us
  local copies, waits for them, and re-layouts: 15.1 us -> 2.3 us
  other arithmetic: 7.1 us -> 0 us
    pallas_call x0 -> x1, Pallas kernels: none -> 68.1 us  [fused(): pl.pallas_call(functools.partial(kernel, sizes, wins), out_shape=jax.Shap...]
    ppermute x10 -> x0, waiting for transfers between devices: 55.8 us -> none  [the longest x4 40.4 us: from_behind(): return lax.ppermute(block, axis, route)]
    ppermute x10 -> x0, starting transfers between devices: 26 us -> none  [the longest x3 12.5 us: with_halo(): before = lax.ppermute(last, axis, up)]
    dot_general x21 -> x0, matrix products: 17.8 us -> none  [the longest x18 11.4 us: causal(): jnp.einsum('frwc,co->frwo', window, matrices[depth_tap, row_tap], preferr...]
    broadcast_in_dim x3 -> x0, local copies, waits for them, and re-layouts: 8.29 us -> none  [the longest x2 8.16 us: body(): grown = jnp.repeat(grown, 2, axis=2)]
    slice x8 -> x0, local copies, waits for them, and re-layouts: 4.15 us -> none  [the longest x3 4 us: column_taps(): padded[:, :, offset:offset + width]]
    concatenate x8 -> x0, other arithmetic: 4.03 us -> none  [the longest x3 1.95 us: column_taps(): jnp.concatenate([padded[:, :, offset:offset + width] for offset in range(...]
    convert_element_type x2 -> x0, other arithmetic: 1.8 us -> none  [the longest x1 1.43 us: body(): first = norm_silu(source, gain_one).astype(jnp.bfloat16)]
  transfers between devices with their start and end apart: 10 -> 0, of which waited for: 10 -> 0; matrix products, arithmetic and copies ran while one was open for 0% -> 0% of each run, Pallas kernels for 0% -> 0%
where the time goes in v1:
time: 71.4 us; the launch traced here: 70.4 us
  Pallas kernels  68.1 us (95%)
  local copies, waits for them, and re-layouts  2.3 us (3%)
    pallas_call x1, Pallas kernels, fused(): pl.pallas_call(functools.partial(kernel, sizes, wins), out_shape=jax.Shap...  68.1 us
    unnamed x1, local copies, waits for them, and re-layouts  2.3 us

profile of v1, /device:TPU:6, one launch (start us, length us, event | category | flops | bytes accessed | tf_op | source)
XLA Modules:
  0.0 70.4 jit_solution(15804002439826948898)
XLA Ops:
  0.0 68.1 %shard_map.64 = bf16[1,16,256,128]{3,2,1,0:T(8,128)(2,1)} custom-call(bf16[1,8,128,256]{3,2,1,0:T(8,128)(2,1)} %latent.1, f32[1,256]{1,0:T(1,128)} %bitcast.2, f32[1,256]{1,0:T(1,128)} %bitcast.3, bf16[3,3,3,256,256]{4,3,2,1,0:T(8,128)(2,1)} %conv_one.1, bf16[3,3,3,256,256]{4,3,2,1,0:T(8,128)(2,1)} %conv_two.1, bf16[3,3,256,128]{3,2,1,0:T(8,128)(2,1)} %up_weight.1), custom_call_target="tpu_custom_call" | custom-call | tf_op jit(solution)/shard_map/pallas_call | solution.py:356
  68.1 2.3 %copy.8 = bf16[1,16,256,128]{3,2,1,0:T(8,128)(2,1)} copy(bf16[1,16,256,128]{3,2,1,0:T(8,128)(2,1)} %shard_map.64) | data formatting | bytes 2097152

commit v2 on v1

v2 whole, which is shorter than its diff:
```python
import functools

import jax
import jax.numpy as jnp
from jax import lax
from jax.experimental import pallas as pl
from jax.experimental.pallas import tpu as pltpu
from jax.sharding import PartitionSpec as P

MESH = pl.DeviceIdType.MESH
PAD = 8


def norm_silu(values, scales):
    mean_sq = jnp.mean(values * values, axis=-1, keepdims=True)
    u = values * lax.rsqrt(mean_sq + 1e-06) * scales
    return 0.5 * u * (1.0 + jnp.tanh(0.5 * u))


def kernel(
    sizes,
    latent,
    gain_one,
    gain_two,
    conv_one,
    conv_two,
    up_weight,
    out,
    lat,
    weights,
    up_raw,
    up_mat,
    held,
    block,
    sums,
    up_sums,
    woven,
    packed,
    load_sem,
    out_sem,
    frame_send,
    frame_recv,
    pair_send,
    pair_recv,
    rim_send,
    rim_recv,
    edge_send,
    edge_recv,
):
    frames, bands = sizes
    height, width, channels = lat.shape
    growth = up_raw.shape[3]
    pairs = height // 2
    tm, rw = lax.axis_index("tm"), lax.axis_index("rows")
    odd = lax.rem(tm, 2)
    mate = (tm + 1 - 2 * odd, rw)
    ahead = (lax.rem(tm + 2, frames), rw)
    behind = (lax.rem(tm + frames - 2, frames), rw)
    above = (tm, lax.rem(rw + bands - 1, bands))
    below = (tm, lax.rem(rw + 1, bands))

    def slot(row):
        return 2 * (row + 1) if row < pairs else 2 * (height - row) + 1

    def rows_of(k):
        return (k, height - 1 - k)

    loads = [pltpu.make_async_copy(latent.at[0], lat, load_sem.at[0])]
    for stage, conv in enumerate((conv_one, conv_two)):
        for e in range(3):
            loads.append(
                pltpu.make_async_copy(
                    conv.at[:, :, e], weights.at[stage, e], load_sem.at[1 + 3 * stage + e]
                )
            )
    loads.append(pltpu.make_async_copy(up_weight, up_raw, load_sem.at[7]))
    for load in loads:
        load.start()

    barrier = pltpu.get_barrier_semaphore()
    for peer in (behind, mate, above, below):
        pl.semaphore_signal(barrier, inc=1, device_id=peer, device_id_type=MESH)

    def remote(src, dst, send, recv, peer):
        return pltpu.make_async_remote_copy(
            src_ref=src, dst_ref=dst, send_sem=send, recv_sem=recv, device_id=peer, device_id_type=MESH
        )

    def to_ahead(s, k):
        both = pl.ds(2 * k + 2, 2)
        return remote(
            held.at[s, 2, both],
            held.at[s, 0, both],
            frame_send.at[s, k],
            frame_recv.at[s, k],
            ahead,
        )

    def to_mate(s, k):
        both = pl.ds(2 * k + 2, 2)
        return remote(
            held.at[s, 2 - 2 * odd, both],
            held.at[s, 1, both],
            pair_send.at[s, k],
            pair_recv.at[s, k],
            mate,
        )

    def to_rims(s, a):
        return [
            remote(
                held.at[s, a, mine],
                held.at[s, a, theirs],
                rim_send.at[s, a, i],
                rim_recv.at[s, a, i],
                peer,
            )
            for i, (mine, theirs, peer) in enumerate(((2, 1, above), (3, 0, below)))
        ]

    def to_edges():
        return [
            remote(block.at[mine], block.at[theirs], edge_send.at[i], edge_recv.at[i], peer)
            for i, (mine, theirs, peer) in enumerate(((2, 1, above), (3, 0, below)))
        ]

    def to_out(k):
        return [
            pltpu.make_async_copy(
                packed.at[pl.ds(2 * row, 2)], out.at[0, pl.ds(2 * row, 2)], out_sem.at[k, i]
            )
            for i, row in enumerate(rows_of(k))
        ]

    def start(copies):
        for copy in copies:
            copy.start()

    def send_own(s, k):
        to_ahead(s, k).start()
        if k == 0:
            start(to_rims(s, 2))

    def take_frame(s, k):
        to_ahead(s, k).wait_recv()

        @pl.when(tm < 2)
        def _():
            held[s, 0, 2 * k + 2 : 2 * k + 4] = jnp.zeros((2, width, channels), held.dtype)

        to_mate(s, k).start()
        if k == 0:
            start(to_rims(s, 0))

    def take_pair(s, k):
        to_mate(s, k).wait_recv()
        if k == 0:
            start(to_rims(s, 1))

    def take_rims(s):
        for a in range(3):
            for copy in to_rims(s, a):
                copy.wait_recv()
        blank = jnp.zeros((3, width, channels), held.dtype)

        @pl.when(rw == 0)
        def _():
            held[s, :, 0] = blank

        @pl.when(rw == bands - 1)
        def _():
            held[s, :, 1] = blank

    def multiply(s, k):
        left = jnp.concatenate(
            [
                jnp.concatenate([held[s, a, slot(row + b - 1)] for row in rows_of(k)], axis=0)
                for a in range(3)
                for b in range(3)
            ],
            axis=1,
        )
        for e in range(3):
            term = jnp.dot(
                left,
                weights[s, e].reshape(9 * channels, channels),
                preferred_element_type=jnp.float32,
            )
            sums[e, :, PAD : PAD + width] = term.reshape(2, width, channels)

    def total(i, lo, n):
        return (
            sums[0, i, PAD + lo - 1 : PAD + lo - 1 + n]
            + sums[1, i, PAD + lo : PAD + lo + n]
            + sums[2, i, PAD + lo + 1 : PAD + lo + 1 + n]
        )

    def settle_one(k):
        for i in range(2):
            for lo in range(0, width, 32):
                value = norm_silu(total(i, lo, 32), gain_two[...])
                held[1, 2, 2 * k + 2 + i, lo : lo + 32] = value.astype(held.dtype)
        send_own(1, k)

    def settle_two(k):
        for i, row in enumerate(rows_of(k)):
            for lo in range(0, width, 32):
                value = lat[row, lo : lo + 32].astype(jnp.float32) + total(i, lo, 32)
                block[2 * k + 2 + i, lo : lo + 32] = value.astype(block.dtype)
        if k == 0:
            start(to_edges())

    def take_edges():
        for copy in to_edges():
            copy.wait_recv()
        blank = jnp.zeros((width, channels), block.dtype)

        @pl.when(rw == 0)
        def _():
            block[0] = blank

        @pl.when(rw == bands - 1)
        def _():
            block[1] = blank

    def upsample(k):
        g = growth
        for p in range(2):
            left = jnp.concatenate(
                [
                    jnp.concatenate([block[slot(row + p + d - 1)] for row in rows_of(k)], axis=0)
                    for d in range(2)
                ],
                axis=1,
            )
            term = jnp.dot(left, up_mat[p], preferred_element_type=jnp.float32)
            up_sums[p, :, PAD : PAD + width] = term.reshape(2, width, 4 * g)
        for p in range(2):
            for i, row in enumerate(rows_of(k)):
                even = (
                    up_sums[p, i, PAD - 1 : PAD - 1 + width, 0:g]
                    + up_sums[p, i, PAD : PAD + width, g : 2 * g]
                )
                odds = (
                    up_sums[p, i, PAD : PAD + width, 2 * g : 3 * g]
                    + up_sums[p, i, PAD + 1 : PAD + 1 + width, 3 * g : 4 * g]
                )
                woven[p, i, pl.ds(0, width, stride=2), :] = even
                woven[p, i, pl.ds(1, width, stride=2), :] = odds
                packed[2 * row + p] = woven[p, i].astype(packed.dtype)
        start(to_out(k))

    loads[0].wait()
    pl.semaphore_wait(barrier, 4)
    for k in range(pairs):
        for i, row in enumerate(rows_of(k)):
            for lo in range(0, width, 32):
                value = norm_silu(lat[row, lo : lo + 32].astype(jnp.float32), gain_one[...])
                held[0, 2, 2 * k + 2 + i, lo : lo + 32] = value.astype(held.dtype)
        send_own(0, k)

    sums[0, :, 0:PAD] = jnp.zeros((2, PAD, channels), jnp.float32)
    sums[2, :, PAD + width :] = jnp.zeros((2, PAD, channels), jnp.float32)
    for p in range(2):
        up_sums[p, :, 0:PAD, 0:growth] = jnp.zeros((2, PAD, growth), jnp.float32)
        up_sums[p, :, PAD + width :, 3 * growth :] = jnp.zeros((2, PAD, growth), jnp.float32)
    loads[7].wait()
    for p, groups in enumerate((((0,), (1, 2)), ((0, 1), (2,)))):
        for d, group in enumerate(groups):
            col = [sum(up_raw[b, e].astype(jnp.float32) for b in group) for e in range(3)]
            parts = (col[0], col[1] + col[2], col[0] + col[1], col[2])
            for j, part in enumerate(parts):
                up_mat[p, d * channels : (d + 1) * channels, j * growth : (j + 1) * growth] = part.astype(
                    up_mat.dtype
                )

    take_frame(0, 0)
    take_pair(0, 0)
    take_frame(0, 1)
    for load in loads[1:4]:
        load.wait()
    take_pair(0, 1)
    take_rims(0)
    for k in range(pairs):
        multiply(0, k)
        if k + 2 < pairs:
            take_frame(0, k + 2)
        if k == pairs - 1:
            take_frame(1, 0)
        settle_one(k)
        if k + 2 < pairs:
            take_pair(0, k + 2)

    take_pair(1, 0)
    take_frame(1, 1)
    for load in loads[4:7]:
        load.wait()
    take_pair(1, 1)
    take_rims(1)
    for k in range(pairs):
        multiply(1, k)
        if k + 2 < pairs:
            take_frame(1, k + 2)
        settle_two(k)
        if k == 1:
            take_edges()
        if k >= 1:
            upsample(k - 1)
        if k + 2 < pairs:
            take_pair(1, k + 2)
    upsample(pairs - 1)

    for s in range(2):
        for k in range(pairs):
            to_ahead(s, k).wait_send()
            to_mate(s, k).wait_send()
        for a in range(3):
            for copy in to_rims(s, a):
                copy.wait_send()
    for copy in to_edges():
        copy.wait_send()
    for k in range(pairs):
        for copy in to_out(k):
            copy.wait()


def fused(sizes, latent, gain_one, conv_one, gain_two, conv_two, up_weight):
    _, height, width, channels = latent.shape
    growth = up_weight.shape[3]
    pairs = height // 2
    dma = pltpu.SemaphoreType.DMA
    bf16, f32 = jnp.bfloat16, jnp.float32
    return pl.pallas_call(
        functools.partial(kernel, sizes),
        out_shape=jax.ShapeDtypeStruct((1, 2 * height, 2 * width, growth), bf16),
        in_specs=[
            pl.BlockSpec(memory_space=pl.ANY),
            pl.BlockSpec(memory_space=pltpu.VMEM),
            pl.BlockSpec(memory_space=pltpu.VMEM),
            pl.BlockSpec(memory_space=pl.ANY),
            pl.BlockSpec(memory_space=pl.ANY),
            pl.BlockSpec(memory_space=pl.ANY),
        ],
        out_specs=pl.BlockSpec(memory_space=pl.ANY),
        scratch_shapes=[
            pltpu.VMEM((height, width, channels), bf16),
            pltpu.VMEM((2, 3, 3, 3, channels, channels), bf16),
            pltpu.VMEM((3, 3, channels, growth), bf16),
            pltpu.VMEM((2, 2 * channels, 4 * growth), bf16),
            pltpu.VMEM((2, 3, height + 2, width, channels), bf16),
            pltpu.VMEM((height + 2, width, channels), bf16),
            pltpu.VMEM((3, 2, width + 2 * PAD, channels), f32),
            pltpu.VMEM((2, 2, width + 2 * PAD, 4 * growth), f32),
            pltpu.VMEM((2, 2, 2 * width, growth), f32),
            pltpu.VMEM((2 * height, 2 * width, growth), bf16),
            dma((8,)),
            dma((pairs, 2)),
            dma((2, pairs)),
            dma((2, pairs)),
            dma((2, pairs)),
            dma((2, pairs)),
            dma((2, 3, 2)),
            dma((2, 3, 2)),
            dma((2,)),
            dma((2,)),
        ],
        compiler_params=pltpu.CompilerParams(
            collective_id=0, has_side_effects=True, vmem_limit_bytes=56 * 1024 * 1024
        ),
    )(
        latent,
        gain_one.reshape(1, channels),
        gain_two.reshape(1, channels),
        conv_one,
        conv_two,
        up_weight,
    )


def solution(mesh):
    sizes = (mesh.shape["tm"], mesh.shape["rows"])
    placed = (P("tm", "rows", None, None), P(), P(), P(), P(), P())
    return jax.shard_map(
        functools.partial(fused, sizes),
        mesh=mesh,
        in_specs=placed,
        out_specs=P("tm", "rows", None, None),
        check_vma=False,
    )
```

time: 71.4 us -> 48.9 us (0.68)
  the two profiles are of different devices: /device:TPU:6 before, /device:TPU:1 now
where the time goes in v2:
time: 48.9 us; the launch traced here: 48.7 us
  Pallas kernels  46.4 us (95%)
  local copies, waits for them, and re-layouts  2.3 us (5%)
    pallas_call x1, Pallas kernels, fused(): pl.pallas_call(functools.partial(kernel, sizes), out_shape=jax.ShapeDtype...  46.4 us
    unnamed x1, local copies, waits for them, and re-layouts  2.3 us

profile of v2, /device:TPU:1, one launch (start us, length us, event | category | flops | bytes accessed | tf_op | source)
XLA Modules:
  0.0 48.7 jit_solution(5301598200935204950)
XLA Ops:
  0.0 46.4 %shard_map.64 = bf16[1,16,256,128]{3,2,1,0:T(8,128)(2,1)} custom-call(bf16[1,8,128,256]{3,2,1,0:T(8,128)(2,1)} %latent.1, f32[1,256]{1,0:T(1,128)} %bitcast.2, f32[1,256]{1,0:T(1,128)} %bitcast.3, bf16[3,3,3,256,256]{4,3,2,1,0:T(8,128)(2,1)} %conv_one.1, bf16[3,3,3,256,256]{4,3,2,1,0:T(8,128)(2,1)} %conv_two.1, bf16[3,3,256,128]{3,2,1,0:T(8,128)(2,1)} %up_weight.1), custom_call_target="tpu_custom_call" | custom-call | tf_op jit(solution)/shard_map/pallas_call | solution.py:333
  46.4 2.3 %copy.8 = bf16[1,16,256,128]{3,2,1,0:T(8,128)(2,1)} copy(bf16[1,16,256,128]{3,2,1,0:T(8,128)(2,1)} %shard_map.64) | data formatting | bytes 2097152

commit v3 on v2

--- a/solution.py
+++ b/solution.py
@@ -35,9 +35,7 @@
     sums,
     up_sums,
     woven,
-    packed,
     load_sem,
-    out_sem,
     frame_send,
     frame_recv,
     pair_send,
@@ -138,6 +136,11 @@
 
     def send_own(s, k):
         to_ahead(s, k).start()
+
+        @pl.when(odd == 0)
+        def _():
+            to_mate(s, k).start()
+
         if k == 0:
             start(to_rims(s, 2))
 
@@ -148,7 +151,10 @@
         def _():
             held[s, 0, 2 * k + 2 : 2 * k + 4] = jnp.zeros((2, width, channels), held.dtype)
 
-        to_mate(s, k).start()
+        @pl.when(odd == 1)
+        def _():
+            to_mate(s, k).start()
+
         if k == 0:
             start(to_rims(s, 0))
 
@@ -157,36 +163,40 @@
         if k == 0:
             start(to_rims(s, 1))
 
-    def take_rims(s):
-        for a in range(3):
+    def take_rims(s, lo, hi):
+        for a in range(lo, hi):
             for copy in to_rims(s, a):
                 copy.wait_recv()
-        blank = jnp.zeros((3, width, channels), held.dtype)
+        blank = jnp.zeros((hi - lo, width, channels), held.dtype)
 
         @pl.when(rw == 0)
         def _():
-            held[s, :, 0] = blank
+            held[s, lo:hi, 0] = blank
 
         @pl.when(rw == bands - 1)
         def _():
-            held[s, :, 1] = blank
-
-    def multiply(s, k):
+            held[s, lo:hi, 1] = blank
+
+    def multiply(s, ks, lo, hi, add):
+        rows = [row for k in ks for row in rows_of(k)]
         left = jnp.concatenate(
             [
-                jnp.concatenate([held[s, a, slot(row + b - 1)] for row in rows_of(k)], axis=0)
-                for a in range(3)
+                jnp.concatenate([held[s, a, slot(row + b - 1)] for row in rows], axis=0)
+                for a in range(lo, hi)
                 for b in range(3)
             ],
             axis=1,
         )
+        here = pl.ds(2 * ks[0], len(rows))
         for e in range(3):
             term = jnp.dot(
                 left,
-                weights[s, e].reshape(9 * channels, channels),
+                weights[s, e, lo:hi].reshape(3 * (hi - lo) * channels, channels),
                 preferred_element_type=jnp.float32,
-            )
-            sums[e, :, PAD : PAD + width] = term.reshape(2, width, channels)
+            ).reshape(len(rows), width, channels)
+            if add:
+                term = term + sums[e, here, PAD : PAD + width]
+            sums[e, here, PAD : PAD + width] = term
 
     def total(i, lo, n):
         return (
@@ -198,14 +208,14 @@
     def settle_one(k):
         for i in range(2):
             for lo in range(0, width, 32):
-                value = norm_silu(total(i, lo, 32), gain_two[...])
+                value = norm_silu(total(2 * k + i, lo, 32), gain_two[...])
                 held[1, 2, 2 * k + 2 + i, lo : lo + 32] = value.astype(held.dtype)
         send_own(1, k)
 
     def settle_two(k):
         for i, row in enumerate(rows_of(k)):
             for lo in range(0, width, 32):
-                value = lat[row, lo : lo + 32].astype(jnp.float32) + total(i, lo, 32)
+                value = lat[row, lo : lo + 32].astype(jnp.float32) + total(2 * k + i, lo, 32)
                 block[2 * k + 2 + i, lo : lo + 32] = value.astype(block.dtype)
         if k == 0:
             start(to_edges())
@@ -247,8 +257,7 @@
                 )
                 woven[p, i, pl.ds(0, width, stride=2), :] = even
                 woven[p, i, pl.ds(1, width, stride=2), :] = odds
-                packed[2 * row + p] = woven[p, i].astype(packed.dtype)
-        start(to_out(k))
+                out[0, 2 * row + p] = woven[p, i].astype(out.dtype)
 
     loads[0].wait()
     pl.semaphore_wait(barrier, 4)
@@ -259,8 +268,8 @@
                 held[0, 2, 2 * k + 2 + i, lo : lo + 32] = value.astype(held.dtype)
         send_own(0, k)
 
-    sums[0, :, 0:PAD] = jnp.zeros((2, PAD, channels), jnp.float32)
-    sums[2, :, PAD + width :] = jnp.zeros((2, PAD, channels), jnp.float32)
+    sums[0, :, 0:PAD] = jnp.zeros((height, PAD, channels), jnp.float32)
+    sums[2, :, PAD + width :] = jnp.zeros((height, PAD, channels), jnp.float32)
     for p in range(2):
         up_sums[p, :, 0:PAD, 0:growth] = jnp.zeros((2, PAD, growth), jnp.float32)
         up_sums[p, :, PAD + width :, 3 * growth :] = jnp.zeros((2, PAD, growth), jnp.float32)
@@ -274,41 +283,54 @@
                     up_mat.dtype
                 )
 
+    for load in loads[1:4]:
+        load.wait()
+    take_rims(0, 2, 3)
+    multiply(0, (0, 1), 2, 3, False)
+    multiply(0, (2, 3), 2, 3, False)
     take_frame(0, 0)
     take_pair(0, 0)
     take_frame(0, 1)
-    for load in loads[1:4]:
-        load.wait()
     take_pair(0, 1)
-    take_rims(0)
-    for k in range(pairs):
-        multiply(0, k)
-        if k + 2 < pairs:
-            take_frame(0, k + 2)
-        if k == pairs - 1:
-            take_frame(1, 0)
-        settle_one(k)
-        if k + 2 < pairs:
-            take_pair(0, k + 2)
-
-    take_pair(1, 0)
-    take_frame(1, 1)
+    take_rims(0, 0, 2)
+    multiply(0, (0,), 0, 2, True)
+    settle_one(0)
+    take_frame(0, 2)
+    take_pair(0, 2)
+    multiply(0, (1,), 0, 2, True)
+    settle_one(1)
+    take_frame(0, 3)
+    take_pair(0, 3)
+    multiply(0, (2, 3), 0, 2, True)
+    settle_one(2)
+    settle_one(3)
+
     for load in loads[4:7]:
         load.wait()
+    take_frame(1, 0)
+    take_pair(1, 0)
+    take_rims(1, 2, 3)
+    multiply(1, (0, 1), 2, 3, False)
+    multiply(1, (2, 3), 2, 3, False)
+    take_frame(1, 1)
     take_pair(1, 1)
-    take_rims(1)
-    for k in range(pairs):
-        multiply(1, k)
-        if k + 2 < pairs:
-            take_frame(1, k + 2)
-        settle_two(k)
-        if k == 1:
-            take_edges()
-        if k >= 1:
-            upsample(k - 1)
-        if k + 2 < pairs:
-            take_pair(1, k + 2)
-    upsample(pairs - 1)
+    take_rims(1, 0, 2)
+    multiply(1, (0,), 0, 2, True)
+    settle_two(0)
+    take_frame(1, 2)
+    take_pair(1, 2)
+    multiply(1, (1,), 0, 2, True)
+    settle_two(1)
+    take_frame(1, 3)
+    take_edges()
+    upsample(0)
+    take_pair(1, 3)
+    multiply(1, (2, 3), 0, 2, True)
+    settle_two(2)
+    upsample(1)
+    settle_two(3)
+    upsample(2)
+    upsample(3)
 
     for s in range(2):
         for k in range(pairs):
@@ -319,9 +341,6 @@
                 copy.wait_send()
     for copy in to_edges():
         copy.wait_send()
-    for k in range(pairs):
-        for copy in to_out(k):
-            copy.wait()
 
 
 def fused(sizes, latent, gain_one, conv_one, gain_two, conv_two, up_weight):
@@ -332,7 +351,7 @@
     bf16, f32 = jnp.bfloat16, jnp.float32
     return pl.pallas_call(
         functools.partial(kernel, sizes),
-        out_shape=jax.ShapeDtypeStruct((1, 2 * height, 2 * width, growth), bf16),
+        out_shape=pltpu.VMEM((1, 2 * height, 2 * width, growth), bf16),
         in_specs=[
             pl.BlockSpec(memory_space=pl.ANY),
             pl.BlockSpec(memory_space=pltpu.VMEM),
@@ -341,7 +360,7 @@
             pl.BlockSpec(memory_space=pl.ANY),
             pl.BlockSpec(memory_space=pl.ANY),
         ],
-        out_specs=pl.BlockSpec(memory_space=pl.ANY),
+        out_specs=pl.BlockSpec(memory_space=pltpu.VMEM),
         scratch_shapes=[
             pltpu.VMEM((height, width, channels), bf16),
             pltpu.VMEM((2, 3, 3, 3, channels, channels), bf16),
@@ -349,12 +368,10 @@
             pltpu.VMEM((2, 2 * channels, 4 * growth), bf16),
             pltpu.VMEM((2, 3, height + 2, width, channels), bf16),
             pltpu.VMEM((height + 2, width, channels), bf16),
-            pltpu.VMEM((3, 2, width + 2 * PAD, channels), f32),
+            pltpu.VMEM((3, height, width + 2 * PAD, channels), f32),
             pltpu.VMEM((2, 2, width + 2 * PAD, 4 * growth), f32),
             pltpu.VMEM((2, 2, 2 * width, growth), f32),
-            pltpu.VMEM((2 * height, 2 * width, growth), bf16),
             dma((8,)),
-            dma((pairs, 2)),
             dma((2, pairs)),
             dma((2, pairs)),
             dma((2, pairs)),

time: 48.9 us -> 40.9 us (0.84)
  the two profiles are of different devices: /device:TPU:1 before, /device:TPU:6 now
where the time goes in v3:
time: 40.9 us; the launch traced here: 40.6 us
  Pallas kernels  39.6 us (97%)
  local copies, waits for them, and re-layouts  0.97 us (2%)
    pallas_call x1, Pallas kernels, fused(): pl.pallas_call(functools.partial(kernel, sizes), out_shape=pltpu.VMEM((1,...  39.6 us
    unnamed x1, local copies, waits for them, and re-layouts  0.97 us

profile of v3, /device:TPU:6, one launch (start us, length us, event | category | flops | bytes accessed | tf_op | source)
XLA Modules:
  0.0 40.6 jit_solution(5524091538103285344)
XLA Ops:
  0.0 39.6 %shard_map.64 = bf16[1,16,256,128]{3,2,1,0:T(8,128)(2,1)S(1)} custom-call(bf16[1,8,128,256]{3,2,1,0:T(8,128)(2,1)} %latent.1, f32[1,256]{1,0:T(1,128)} %bitcast.2, f32[1,256]{1,0:T(1,128)} %bitcast.3, bf16[3,3,3,256,256]{4,3,2,1,0:T(8,128)(2,1)} %conv_one.1, bf16[3,3,3,256,256]{4,3,2,1,0:T(8,128)(2,1)} %conv_two.1, bf16[3,3,256,128]{3,2,1,0:T(8,128)(2,1)} %up_weight.1), custom_call_target="tpu_custom_call" | custom-call | tf_op jit(solution)/shard_map/pallas_call | solution.py:352
  39.6 1.0 %copy.8 = bf16[1,16,256,128]{3,2,1,0:T(8,128)(2,1)} copy(bf16[1,16,256,128]{3,2,1,0:T(8,128)(2,1)S(1)} %shard_map.64) | data formatting | bytes 2097152

commit v4 on v3

--- a/solution.py
+++ b/solution.py
@@ -56,6 +56,8 @@
     behind = (lax.rem(tm + frames - 2, frames), rw)
     above = (tm, lax.rem(rw + bands - 1, bands))
     below = (tm, lax.rem(rw + 1, bands))
+    has_ahead, has_behind = tm < frames - 2, tm >= 2
+    has_above, has_below = rw > 0, rw < bands - 1
 
     def slot(row):
         return 2 * (row + 1) if row < pairs else 2 * (height - row) + 1
@@ -76,8 +78,12 @@
         load.start()
 
     barrier = pltpu.get_barrier_semaphore()
-    for peer in (behind, mate, above, below):
-        pl.semaphore_signal(barrier, inc=1, device_id=peer, device_id_type=MESH)
+    pl.semaphore_signal(barrier, inc=1, device_id=mate, device_id_type=MESH)
+    for ok, peer in ((has_behind, behind), (has_above, above), (has_below, below)):
+
+        @pl.when(ok)
+        def _(peer=peer):
+            pl.semaphore_signal(barrier, inc=1, device_id=peer, device_id_type=MESH)
 
     def remote(src, dst, send, recv, peer):
         return pltpu.make_async_remote_copy(
@@ -134,48 +140,54 @@
         for copy in copies:
             copy.start()
 
+    def to_rows(copies, act):
+        for copy, ok in zip(copies, (has_above, has_below)):
+
+            @pl.when(ok)
+            def _(copy=copy):
+                act(copy)
+
+    def send_rows(copies):
+        to_rows(copies, lambda copy: copy.start())
+
+    def drain_rows(copies):
+        to_rows(copies, lambda copy: copy.wait_send())
+
+    def take_rows(copies):
+        to_rows(copies[::-1], lambda copy: copy.wait_recv())
+
     def send_own(s, k):
-        to_ahead(s, k).start()
+        @pl.when(has_ahead)
+        def _():
+            to_ahead(s, k).start()
 
         @pl.when(odd == 0)
         def _():
             to_mate(s, k).start()
 
         if k == 0:
-            start(to_rims(s, 2))
+            send_rows(to_rims(s, 2))
 
     def take_frame(s, k):
-        to_ahead(s, k).wait_recv()
-
-        @pl.when(tm < 2)
+        @pl.when(has_behind)
         def _():
-            held[s, 0, 2 * k + 2 : 2 * k + 4] = jnp.zeros((2, width, channels), held.dtype)
+            to_ahead(s, k).wait_recv()
 
         @pl.when(odd == 1)
         def _():
             to_mate(s, k).start()
 
         if k == 0:
-            start(to_rims(s, 0))
+            send_rows(to_rims(s, 0))
 
     def take_pair(s, k):
         to_mate(s, k).wait_recv()
         if k == 0:
-            start(to_rims(s, 1))
+            send_rows(to_rims(s, 1))
 
     def take_rims(s, lo, hi):
         for a in range(lo, hi):
-            for copy in to_rims(s, a):
-                copy.wait_recv()
-        blank = jnp.zeros((hi - lo, width, channels), held.dtype)
-
-        @pl.when(rw == 0)
-        def _():
-            held[s, lo:hi, 0] = blank
-
-        @pl.when(rw == bands - 1)
-        def _():
-            held[s, lo:hi, 1] = blank
+            take_rows(to_rims(s, a))
 
     def multiply(s, ks, lo, hi, add):
         rows = [row for k in ks for row in rows_of(k)]
@@ -218,35 +230,24 @@
                 value = lat[row, lo : lo + 32].astype(jnp.float32) + total(2 * k + i, lo, 32)
                 block[2 * k + 2 + i, lo : lo + 32] = value.astype(block.dtype)
         if k == 0:
-            start(to_edges())
-
-    def take_edges():
-        for copy in to_edges():
-            copy.wait_recv()
-        blank = jnp.zeros((width, channels), block.dtype)
-
-        @pl.when(rw == 0)
-        def _():
-            block[0] = blank
-
-        @pl.when(rw == bands - 1)
-        def _():
-            block[1] = blank
-
-    def upsample(k):
+            send_rows(to_edges())
+
+    def upsample(*ks):
         g = growth
+        rows = [row for k in ks for row in rows_of(k)]
+        n = len(rows)
         for p in range(2):
             left = jnp.concatenate(
                 [
-                    jnp.concatenate([block[slot(row + p + d - 1)] for row in rows_of(k)], axis=0)
+                    jnp.concatenate([block[slot(row + p + d - 1)] for row in rows], axis=0)
                     for d in range(2)
                 ],
                 axis=1,
             )
             term = jnp.dot(left, up_mat[p], preferred_element_type=jnp.float32)
-            up_sums[p, :, PAD : PAD + width] = term.reshape(2, width, 4 * g)
+            up_sums[p, 0:n, PAD : PAD + width] = term.reshape(n, width, 4 * g)
         for p in range(2):
-            for i, row in enumerate(rows_of(k)):
+            for i, row in enumerate(rows):
                 even = (
                     up_sums[p, i, PAD - 1 : PAD - 1 + width, 0:g]
                     + up_sums[p, i, PAD : PAD + width, g : 2 * g]
@@ -260,7 +261,8 @@
                 out[0, 2 * row + p] = woven[p, i].astype(out.dtype)
 
     loads[0].wait()
-    pl.semaphore_wait(barrier, 4)
+    peers = 1 + sum(ok.astype(jnp.int32) for ok in (has_ahead, has_above, has_below))
+    pl.semaphore_wait(barrier, peers)
     for k in range(pairs):
         for i, row in enumerate(rows_of(k)):
             for lo in range(0, width, 32):
@@ -268,11 +270,22 @@
                 held[0, 2, 2 * k + 2 + i, lo : lo + 32] = value.astype(held.dtype)
         send_own(0, k)
 
+    for ok, place in ((has_above, 0), (has_below, 1)):
+
+        @pl.when(jnp.logical_not(ok))
+        def _(place=place):
+            held[:, :, place] = jnp.zeros((2, 3, width, channels), held.dtype)
+            block[place] = jnp.zeros((width, channels), block.dtype)
+
+    @pl.when(jnp.logical_not(has_behind))
+    def _():
+        held[:, 0, 2:] = jnp.zeros((2, height, width, channels), held.dtype)
+
     sums[0, :, 0:PAD] = jnp.zeros((height, PAD, channels), jnp.float32)
     sums[2, :, PAD + width :] = jnp.zeros((height, PAD, channels), jnp.float32)
     for p in range(2):
-        up_sums[p, :, 0:PAD, 0:growth] = jnp.zeros((2, PAD, growth), jnp.float32)
-        up_sums[p, :, PAD + width :, 3 * growth :] = jnp.zeros((2, PAD, growth), jnp.float32)
+        up_sums[p, :, 0:PAD, 0:growth] = jnp.zeros((6, PAD, growth), jnp.float32)
+        up_sums[p, :, PAD + width :, 3 * growth :] = jnp.zeros((6, PAD, growth), jnp.float32)
     loads[7].wait()
     for p, groups in enumerate((((0,), (1, 2)), ((0, 1), (2,)))):
         for d, group in enumerate(groups):
@@ -291,17 +304,21 @@
     take_frame(0, 0)
     take_pair(0, 0)
     take_frame(0, 1)
+    take_rims(0, 0, 1)
+    multiply(0, (0,), 0, 1, True)
     take_pair(0, 1)
-    take_rims(0, 0, 2)
-    multiply(0, (0,), 0, 2, True)
+    take_rims(0, 1, 2)
+    multiply(0, (0,), 1, 2, True)
     settle_one(0)
     take_frame(0, 2)
+    multiply(0, (1,), 0, 1, True)
     take_pair(0, 2)
-    multiply(0, (1,), 0, 2, True)
+    multiply(0, (1,), 1, 2, True)
     settle_one(1)
     take_frame(0, 3)
+    multiply(0, (2, 3), 0, 1, True)
     take_pair(0, 3)
-    multiply(0, (2, 3), 0, 2, True)
+    multiply(0, (2, 3), 1, 2, True)
     settle_one(2)
     settle_one(3)
 
@@ -322,25 +339,26 @@
     multiply(1, (1,), 0, 2, True)
     settle_two(1)
     take_frame(1, 3)
-    take_edges()
+    multiply(1, (2, 3), 0, 1, True)
+    take_rows(to_edges())
     upsample(0)
     take_pair(1, 3)
-    multiply(1, (2, 3), 0, 2, True)
+    multiply(1, (2, 3), 1, 2, True)
     settle_two(2)
-    upsample(1)
     settle_two(3)
-    upsample(2)
-    upsample(3)
+    upsample(1, 2, 3)
 
     for s in range(2):
         for k in range(pairs):
-            to_ahead(s, k).wait_send()
+
+            @pl.when(has_ahead)
+            def _(s=s, k=k):
+                to_ahead(s, k).wait_send()
+
             to_mate(s, k).wait_send()
         for a in range(3):
-            for copy in to_rims(s, a):
-                copy.wait_send()
-    for copy in to_edges():
-        copy.wait_send()
+            drain_rows(to_rims(s, a))
+    drain_rows(to_edges())
 
 
 def fused(sizes, latent, gain_one, conv_one, gain_two, conv_two, up_weight):
@@ -369,8 +387,8 @@
             pltpu.VMEM((2, 3, height + 2, width, channels), bf16),
             pltpu.VMEM((height + 2, width, channels), bf16),
             pltpu.VMEM((3, height, width + 2 * PAD, channels), f32),
-            pltpu.VMEM((2, 2, width + 2 * PAD, 4 * growth), f32),
-            pltpu.VMEM((2, 2, 2 * width, growth), f32),
+            pltpu.VMEM((2, 6, width + 2 * PAD, 4 * growth), f32),
+            pltpu.VMEM((2, 6, 2 * width, growth), f32),
             dma((8,)),
             dma((2, pairs)),
             dma((2, pairs)),

time: 40.9 us -> 37.2 us (0.910)
  Pallas kernels: 39.6 us -> 35.7 us
    pallas_call x1, Pallas kernels: 39.6 us -> 35.7 us  [fused(): pl.pallas_call(functools.partial(kernel, sizes), out_shape=pltpu.VMEM((1,...]
where the time goes in v4:
time: 37.2 us; the launch traced here: 36.6 us
  Pallas kernels  35.7 us (96%)
  local copies, waits for them, and re-layouts  0.97 us (3%)
    pallas_call x1, Pallas kernels, fused(): pl.pallas_call(functools.partial(kernel, sizes), out_shape=pltpu.VMEM((1,...  35.7 us
    unnamed x1, local copies, waits for them, and re-layouts  0.97 us

profile of v4, /device:TPU:6, one launch (start us, length us, event | category | flops | bytes accessed | tf_op | source)
XLA Modules:
  0.0 36.6 jit_solution(3849650559190567464)
XLA Ops:
  0.0 35.7 %shard_map.64 = bf16[1,16,256,128]{3,2,1,0:T(8,128)(2,1)S(1)} custom-call(bf16[1,8,128,256]{3,2,1,0:T(8,128)(2,1)} %latent.1, f32[1,256]{1,0:T(1,128)} %bitcast.2, f32[1,256]{1,0:T(1,128)} %bitcast.3, bf16[3,3,3,256,256]{4,3,2,1,0:T(8,128)(2,1)} %conv_one.1, bf16[3,3,3,256,256]{4,3,2,1,0:T(8,128)(2,1)} %conv_two.1, bf16[3,3,256,128]{3,2,1,0:T(8,128)(2,1)} %up_weight.1), custom_call_target="tpu_custom_call" | custom-call | tf_op jit(solution)/shard_map/pallas_call | solution.py:370
  35.7 1.0 %copy.8 = bf16[1,16,256,128]{3,2,1,0:T(8,128)(2,1)} copy(bf16[1,16,256,128]{3,2,1,0:T(8,128)(2,1)S(1)} %shard_map.64) | data formatting | bytes 2097152

commit v5 on v4

--- a/solution.py
+++ b/solution.py
@@ -284,8 +284,8 @@
     sums[0, :, 0:PAD] = jnp.zeros((height, PAD, channels), jnp.float32)
     sums[2, :, PAD + width :] = jnp.zeros((height, PAD, channels), jnp.float32)
     for p in range(2):
-        up_sums[p, :, 0:PAD, 0:growth] = jnp.zeros((6, PAD, growth), jnp.float32)
-        up_sums[p, :, PAD + width :, 3 * growth :] = jnp.zeros((6, PAD, growth), jnp.float32)
+        up_sums[p, :, 0:PAD, 0:growth] = jnp.zeros((8, PAD, growth), jnp.float32)
+        up_sums[p, :, PAD + width :, 3 * growth :] = jnp.zeros((8, PAD, growth), jnp.float32)
     loads[7].wait()
     for p, groups in enumerate((((0,), (1, 2)), ((0, 1), (2,)))):
         for d, group in enumerate(groups):
@@ -330,23 +330,26 @@
     multiply(1, (0, 1), 2, 3, False)
     multiply(1, (2, 3), 2, 3, False)
     take_frame(1, 1)
+    take_rims(1, 0, 1)
+    multiply(1, (0,), 0, 1, True)
     take_pair(1, 1)
-    take_rims(1, 0, 2)
-    multiply(1, (0,), 0, 2, True)
+    take_rims(1, 1, 2)
+    multiply(1, (0,), 1, 2, True)
     settle_two(0)
     take_frame(1, 2)
+    multiply(1, (1,), 0, 1, True)
     take_pair(1, 2)
-    multiply(1, (1,), 0, 2, True)
+    multiply(1, (1,), 1, 2, True)
     settle_two(1)
     take_frame(1, 3)
     multiply(1, (2, 3), 0, 1, True)
-    take_rows(to_edges())
-    upsample(0)
     take_pair(1, 3)
     multiply(1, (2, 3), 1, 2, True)
     settle_two(2)
     settle_two(3)
     upsample(1, 2, 3)
+    take_rows(to_edges())
+    upsample(0)
 
     for s in range(2):
         for k in range(pairs):
@@ -387,8 +390,8 @@
             pltpu.VMEM((2, 3, height + 2, width, channels), bf16),
             pltpu.VMEM((height + 2, width, channels), bf16),
             pltpu.VMEM((3, height, width + 2 * PAD, channels), f32),
-            pltpu.VMEM((2, 6, width + 2 * PAD, 4 * growth), f32),
-            pltpu.VMEM((2, 6, 2 * width, growth), f32),
+            pltpu.VMEM((2, 8, width + 2 * PAD, 4 * growth), f32),
+            pltpu.VMEM((2, 8, 2 * width, growth), f32),
             dma((8,)),
             dma((2, pairs)),
             dma((2, pairs)),

time: 37.2 us -> 35.2 us (0.946)
  Pallas kernels: 35.7 us -> 33.9 us
    pallas_call x1, Pallas kernels: 35.7 us -> 33.9 us  [fused(): pl.pallas_call(functools.partial(kernel, sizes), out_shape=pltpu.VMEM((1,...]
where the time goes in v5:
time: 35.2 us; the launch traced here: 34.9 us
  Pallas kernels  33.9 us (96%)
  local copies, waits for them, and re-layouts  0.97 us (3%)
    pallas_call x1, Pallas kernels, fused(): pl.pallas_call(functools.partial(kernel, sizes), out_shape=pltpu.VMEM((1,...  33.9 us
    unnamed x1, local copies, waits for them, and re-layouts  0.97 us

profile of v5, /device:TPU:6, one launch (start us, length us, event | category | flops | bytes accessed | tf_op | source)
XLA Modules:
  0.0 34.9 jit_solution(2230246596735701179)
XLA Ops:
  0.0 33.9 %shard_map.64 = bf16[1,16,256,128]{3,2,1,0:T(8,128)(2,1)S(1)} custom-call(bf16[1,8,128,256]{3,2,1,0:T(8,128)(2,1)} %latent.1, f32[1,256]{1,0:T(1,128)} %bitcast.2, f32[1,256]{1,0:T(1,128)} %bitcast.3, bf16[3,3,3,256,256]{4,3,2,1,0:T(8,128)(2,1)} %conv_one.1, bf16[3,3,3,256,256]{4,3,2,1,0:T(8,128)(2,1)} %conv_two.1, bf16[3,3,256,128]{3,2,1,0:T(8,128)(2,1)} %up_weight.1), custom_call_target="tpu_custom_call" | custom-call | tf_op jit(solution)/shard_map/pallas_call | solution.py:373
  33.9 1.0 %copy.8 = bf16[1,16,256,128]{3,2,1,0:T(8,128)(2,1)} copy(bf16[1,16,256,128]{3,2,1,0:T(8,128)(2,1)S(1)} %shard_map.64) | data formatting | bytes 2097152

commit v6 on v5

--- a/solution.py
+++ b/solution.py
@@ -9,6 +9,7 @@
 
 MESH = pl.DeviceIdType.MESH
 PAD = 8
+RING = 8
 
 
 def norm_silu(values, scales):
@@ -44,6 +45,9 @@
     rim_recv,
     edge_send,
     edge_recv,
+    passing,
+    relay_send,
+    relay_recv,
 ):
     frames, bands = sizes
     height, width, channels = lat.shape
@@ -57,6 +61,14 @@
     above = (tm, lax.rem(rw + bands - 1, bands))
     below = (tm, lax.rem(rw + 1, bands))
     has_ahead, has_behind = tm < frames - 2, tm >= 2
+    turn = lax.rem(tm, RING)
+    down = (tm - turn + lax.rem(turn + RING - 2, RING), rw)
+    up = (tm - turn + lax.rem(turn + 2, RING), rw)
+    leaves, enters = turn // 2 == 1, turn // 2 == 0
+    far_out = (lax.rem(tm + RING - 2, frames), rw)
+    far_in = (lax.rem(tm + frames - RING + 2, frames), rw)
+    has_out = jnp.logical_and(leaves, tm < frames - RING)
+    has_in = jnp.logical_and(enters, tm >= RING)
     has_above, has_below = rw > 0, rw < bands - 1
 
     def slot(row):
@@ -79,7 +91,13 @@
 
     barrier = pltpu.get_barrier_semaphore()
     pl.semaphore_signal(barrier, inc=1, device_id=mate, device_id_type=MESH)
-    for ok, peer in ((has_behind, behind), (has_above, above), (has_below, below)):
+    pl.semaphore_signal(barrier, inc=1, device_id=up, device_id_type=MESH)
+    for ok, peer in (
+        (has_behind, behind),
+        (has_in, far_in),
+        (has_above, above),
+        (has_below, below),
+    ):
 
         @pl.when(ok)
         def _(peer=peer):
@@ -90,8 +108,14 @@
             src_ref=src, dst_ref=dst, send_sem=send, recv_sem=recv, device_id=peer, device_id_type=MESH
         )
 
+    def relay(step, peer):
+        last = height + 1
+        src = (held.at[0, 2, last], passing.at[0], passing.at[1])[step]
+        dst = (passing.at[0], passing.at[1], held.at[0, 0, last])[step]
+        return remote(src, dst, relay_send.at[step], relay_recv.at[step], peer)
+
     def to_ahead(s, k):
-        both = pl.ds(2 * k + 2, 2)
+        both = pl.ds(2 * k + 2, 1 if s == 0 and k == pairs - 1 else 2)
         return remote(
             held.at[s, 2, both],
             held.at[s, 0, both],
@@ -156,6 +180,15 @@
     def take_rows(copies):
         to_rows(copies[::-1], lambda copy: copy.wait_recv())
 
+    def when(ok, act):
+        @pl.when(ok)
+        def _():
+            act()
+
+    def pass_out(act):
+        when(jnp.logical_not(leaves), lambda: act(relay(2, down)))
+        when(has_out, lambda: act(relay(2, far_out)))
+
     def send_own(s, k):
         @pl.when(has_ahead)
         def _():
@@ -172,6 +205,8 @@
         @pl.when(has_behind)
         def _():
             to_ahead(s, k).wait_recv()
+            if s == 0 and k == pairs - 1:
+                relay(2, down).wait_recv()
 
         @pl.when(odd == 1)
         def _():
@@ -261,14 +296,18 @@
                 out[0, 2 * row + p] = woven[p, i].astype(out.dtype)
 
     loads[0].wait()
-    peers = 1 + sum(ok.astype(jnp.int32) for ok in (has_ahead, has_above, has_below))
+    peers = 2 + sum(ok.astype(jnp.int32) for ok in (has_ahead, has_out, has_above, has_below))
     pl.semaphore_wait(barrier, peers)
-    for k in range(pairs):
+    for k in (0, 3, 1, 2):
         for i, row in enumerate(rows_of(k)):
             for lo in range(0, width, 32):
                 value = norm_silu(lat[row, lo : lo + 32].astype(jnp.float32), gain_one[...])
                 held[0, 2, 2 * k + 2 + i, lo : lo + 32] = value.astype(held.dtype)
-        send_own(0, k)
+        if k == pairs - 1:
+            relay(0, down).start()
+        else:
+            send_own(0, k)
+    send_own(0, pairs - 1)
 
     for ok, place in ((has_above, 0), (has_below, 1)):
 
@@ -301,11 +340,15 @@
     take_rims(0, 2, 3)
     multiply(0, (0, 1), 2, 3, False)
     multiply(0, (2, 3), 2, 3, False)
+    relay(0, down).wait_recv()
+    relay(1, down).start()
     take_frame(0, 0)
     take_pair(0, 0)
     take_frame(0, 1)
     take_rims(0, 0, 1)
     multiply(0, (0,), 0, 1, True)
+    relay(1, down).wait_recv()
+    pass_out(lambda copy: copy.start())
     take_pair(0, 1)
     take_rims(0, 1, 2)
     multiply(0, (0,), 1, 2, True)
@@ -351,6 +394,9 @@
     take_rows(to_edges())
     upsample(0)
 
+    relay(0, down).wait_send()
+    relay(1, down).wait_send()
+    pass_out(lambda copy: copy.wait_send())
     for s in range(2):
         for k in range(pairs):
 
@@ -401,6 +447,9 @@
             dma((2, 3, 2)),
             dma((2,)),
             dma((2,)),
+            pltpu.VMEM((2, width, channels), bf16),
+            dma((3,)),
+            dma((3,)),
         ],
         compiler_params=pltpu.CompilerParams(
             collective_id=0, has_side_effects=True, vmem_limit_bytes=56 * 1024 * 1024

time: 35.2 us -> 35 us (level)
  no operation moved by 1% of the time
where the time goes in v6:
time: 35 us
  Pallas kernels  34 us (97%)
  local copies, waits for them, and re-layouts  0.97 us (3%)
    pallas_call x1, Pallas kernels, fused(): pl.pallas_call(functools.partial(kernel, sizes), out_shape=pltpu.VMEM((1,...  34 us
    unnamed x1, local copies, waits for them, and re-layouts  0.97 us

profile of v6, /device:TPU:6, one launch (start us, length us, event | category | flops | bytes accessed | tf_op | source)
XLA Modules:
  0.0 35.0 jit_solution(16584918047385829941)
XLA Ops:
  0.0 34.0 %shard_map.64 = bf16[1,16,256,128]{3,2,1,0:T(8,128)(2,1)S(1)} custom-call(bf16[1,8,128,256]{3,2,1,0:T(8,128)(2,1)} %latent.1, f32[1,256]{1,0:T(1,128)} %bitcast.2, f32[1,256]{1,0:T(1,128)} %bitcast.3, bf16[3,3,3,256,256]{4,3,2,1,0:T(8,128)(2,1)} %conv_one.1, bf16[3,3,3,256,256]{4,3,2,1,0:T(8,128)(2,1)} %conv_two.1, bf16[3,3,256,128]{3,2,1,0:T(8,128)(2,1)} %up_weight.1), custom_call_target="tpu_custom_call" | custom-call | tf_op jit(solution)/shard_map/pallas_call | solution.py:419
  34.0 1.0 %copy.8 = bf16[1,16,256,128]{3,2,1,0:T(8,128)(2,1)} copy(bf16[1,16,256,128]{3,2,1,0:T(8,128)(2,1)S(1)} %shard_map.64) | data formatting | bytes 2097152
